TPU v7x, 256 devices: a whole 4x4x8 slice. The times are simulated.
256 devices in a mesh: dp: 128 (over x, y_hi, z, core), mp: 2 (over y_lo).
Axes of the slice: x: 4, y: 4 (y_hi: 2, y_lo: 2; y = y_hi * 2 + y_lo), z: 8, core: 2. Of those that a mesh axis runs over, the one named last changes fastest.
Arguments:
- picture_vectors: bfloat16 [131072, 1152], P('dp', 'mp'), may hold values from -5 to 5
- caption_vectors: bfloat16 [131072, 1152], P('dp', 'mp'), may hold values from -5 to 5
- sharpness_coefficient: float32 [1], replicated, may hold values from 4 to 8
- affinity_offset: float32 [1], replicated, may hold values from -4 to -2
Outputs:
- image_grad: float32 [131072, 1152], P('dp', 'mp')
- caption_vectors_derivative: float32 [131072, 1152], P('dp', 'mp')
- row_loss: float32 [131072], P(('dp', 'mp'))
All inputs are finite; a program needn't handle non-finite values.
Results may differ from a plain program's by a relative error of at most 0.0045.
Values may be sent and summed in bfloat16 or wider, within the bound.
A program may use at most 128 MiB of HBM per device.

v0:
```python
import jax
import jax.numpy as jnp
from jax import lax
from jax.sharding import PartitionSpec as P

epsilon = 1e-06


def shifted(block, axis, distance):
    devices = range(lax.axis_size(axis))
    route = [((i - distance) % len(devices), i) for i in devices]
    return lax.ppermute(block, axis, route)


def per_device(picture_vectors, caption_vectors, sharpness_coefficient, affinity_offset):
    row_count = picture_vectors.shape[0]
    share_rows = row_count // lax.axis_size("mp")
    image_float = picture_vectors.astype(jnp.float32)
    text_float = caption_vectors.astype(jnp.float32)
    image_square, text_square = lax.psum(
        (jnp.sum(image_float * image_float, axis=1), jnp.sum(text_float * text_float, axis=1)), "mp"
    )
    image_inverse = lax.rsqrt(image_square + epsilon)
    text_inverse = lax.rsqrt(text_square + epsilon)
    image_unit = (image_float * image_inverse[:, None]).astype(jnp.bfloat16)
    text_unit = (text_float * text_inverse[:, None]).astype(jnp.bfloat16)
    image_rows = lax.all_to_all(image_unit, "mp", split_axis=0, concat_axis=1, tiled=True)
    text_full = lax.all_gather(text_unit, "mp", axis=1, tiled=True)
    preceding_text_rows = shifted(text_full, "dp", 1)
    multiplier_amount = sharpness_coefficient[0]
    block_shift = affinity_offset[0]
    local_logit_block = (
        multiplier_amount
        * jnp.einsum("ik,jk->ij", image_rows, text_full, preferred_element_type=jnp.float32)
        + block_shift
    )
    preceding_logit_block = (
        multiplier_amount
        * jnp.einsum(
            "ik,jk->ij", image_rows, preceding_text_rows, preferred_element_type=jnp.float32
        )
        + block_shift
    )
    first_row = lax.axis_index("mp") * share_rows
    row_index = lax.broadcasted_iota(jnp.int32, local_logit_block.shape, 0) + first_row
    col_index = lax.broadcasted_iota(jnp.int32, local_logit_block.shape, 1)
    local_label_sign = jnp.where(row_index == col_index, jnp.float32(1.0), jnp.float32(-1.0))
    row_loss = (
        jnp.sum(jax.nn.softplus(-local_label_sign * local_logit_block), axis=1)
        + jnp.sum(jax.nn.softplus(preceding_logit_block), axis=1)
    ) / (2 * row_count)
    local_block_weight = (
        multiplier_amount
        * -local_label_sign
        * jax.nn.sigmoid(-local_label_sign * local_logit_block)
    ).astype(jnp.bfloat16)
    preceding_block_weight = (multiplier_amount * jax.nn.sigmoid(preceding_logit_block)).astype(
        jnp.bfloat16
    )
    image_partial = jnp.dot(
        local_block_weight, text_full, preferred_element_type=jnp.float32
    ) + jnp.dot(preceding_block_weight, preceding_text_rows, preferred_element_type=jnp.float32)
    image_back = image_rows.astype(jnp.float32)
    image_dot = jnp.sum(image_back * image_partial, axis=1)
    share_inverse = lax.dynamic_slice_in_dim(image_inverse, first_row, share_rows, 0)
    image_local = (image_partial - image_back * image_dot[:, None]) * share_inverse[:, None]
    image_grad = lax.all_to_all(image_local, "mp", split_axis=1, concat_axis=0, tiled=True)
    text_own = jnp.einsum(
        "ij,ik->jk", local_block_weight, image_rows, preferred_element_type=jnp.float32
    )
    text_far = jnp.einsum(
        "ij,ik->jk", preceding_block_weight, image_rows, preferred_element_type=jnp.float32
    )
    text_home = shifted(text_far.astype(jnp.bfloat16), "dp", -1).astype(text_far.dtype)
    text_total = lax.psum_scatter(text_own + text_home, "mp", scatter_dimension=1, tiled=True)
    text_back = text_unit.astype(jnp.float32)
    text_dot = lax.psum(jnp.sum(text_back * text_total, axis=1), "mp")
    caption_vectors_derivative = (text_total - text_back * text_dot[:, None]) * text_inverse[
        :, None
    ]
    return (image_grad, caption_vectors_derivative, row_loss)


def solution(mesh):
    placed = (P("dp", "mp"), P("dp", "mp"), P(), P())
    return jax.shard_map(
        per_device,
        mesh=mesh,
        in_specs=placed,
        out_specs=(P("dp", "mp"), P("dp", "mp"), P(("dp", "mp"))),
        check_vma=False,
    )
```

profile of v0, /device:TPU:1, one launch (start us, length us, event | category | flops | bytes accessed | tf_op | source)
XLA Modules:
  0.0 250.0 jit_solution(14434211992691122016)
XLA Ops:
  7.2 2.2 fusion
  9.5 4.6 %all-reduce = (f32[1024]{0:T(1024)S(1)}, f32[1024]{0:T(1024)S(1)}) all-reduce(f32[1024]{0:T(1024)S(1)} %get-tuple-element.12, f32[1024]{0:T(1024)S(1)} %get-tuple-element.11), channel_id=1, replica_groups=mesh['dp'=128,'mp'=2] {'mp'}, use_global_device_ids=true, to_apply=%region_3.0 | all-reduce | flops 2048 | bytes 16384 | tf_op jit(solution)/shard_map/psum | solution.py:20
  14.1 1.3 fusion.3
  15.5 45.6 %all-gather.2.cloned.1.call-done = bf16[1024,1152]{0,1:T(8,128)(2,1)} async-done(((bf16[1024,576]{0,1:T(8,128)(2,1)}), bf16[1024,1152]{0,1:T(8,128)(2,1)}) %all-gather.2.cloned.1.call-update) | async-done | bytes 2359312 | tf_op jit(solution)/shard_map/all_gather | solution.py:28
  61.1 1.8 collective-permute-start
  63.2 1.1 copy.27
  64.3 3.6 %all-to-all-start = ((bf16[2,512,576]{1,2,0:T(8,128)(2,1)}), bf16[2,512,576]{1,2,0:T(8,128)(2,1)S(1)}, u32[]{:S(2)}, u32[]{:S(2)}) async-start(bf16[2,512,576]{1,2,0:T(8,128)(2,1)} %bitcast.20), calls=%async_computation | async-start | bytes 2359296 | tf_op jit(solution)/shard_map/all_to_all | solution.py:27
  69.3 36.2 %all-to-all-done = bf16[2,512,576]{1,2,0:T(8,128)(2,1)S(1)} async-done(((bf16[2,512,576]{1,2,0:T(8,128)(2,1)}), bf16[2,512,576]{1,2,0:T(8,128)(2,1)S(1)}, u32[]{:S(2)}, u32[]{:S(2)}) %all-to-all-start) | async-done | bytes 1179680 | tf_op jit(solution)/shard_map/all_to_all | solution.py:27
  105.4 4.3 %fusion.11 = (f32[512]{0:T(512)S(1)}, f32[512,1024]{1,0:T(8,128)S(1)}) fusion(f32[]{:T(128)} %bitcast.28, f32[]{:T(128)} %bitcast.23, bf16[512,1152]{0,1:T(8,128)(2,1)S(1)} %bitcast.33, bf16[1024,1152]{0,1:T(8,128)(2,1)} %collective-permute-done), kind=kOutput, calls=%fused_computation.24 | convolution fusion | flops 1212677632 | bytes 5638152 | tf_op jit(solution)/shard_map/ik,jk->ij/dot_general | solution.py:39
  109.8 2.9 %convolution_convert_fusion = bf16[1024,1152]{0,1:T(8,128)(2,1)} fusion(bf16[512,1152]{0,1:T(8,128)(2,1)S(1)} %bitcast.34, f32[512,1024]{1,0:T(8,128)S(1)} %get-tuple-element.10, f32[]{:T(128)} %bitcast.30, f32[]{:T(128)} %bitcast.25), kind=kOutput, calls=%fused_computation.3 | convolution fusion | flops 1212809216 | bytes 5636104 | tf_op jit(solution)/shard_map/ij,ik->jk/dot_general | solution.py:71
  113.1 5.2 %fusion.10 = (f32[512]{0:T(512)}, f32[512,1024]{1,0:T(8,128)S(1)}) fusion(f32[]{:T(128)} %bitcast.27, bf16[512,1152]{0,1:T(8,128)(2,1)S(1)} %bitcast.35, bf16[1024,1152]{0,1:T(8,128)(2,1)} %all-gather.2.cloned.1.call-done, f32[]{:T(128)} %bitcast.24, s32[512]{0:T(512)S(1)} %iota_add_fusion), kind=kOutput, calls=%fused_computation.23 | convolution fusion | flops 1214774784 | bytes 5640200 | tf_op jit(solution)/shard_map/ik,jk->ij/dot_general | solution.py:34
  118.3 22.9 %collective-permute-done.1 = bf16[1024,1152]{0,1:T(8,128)(2,1)} collective-permute-done((bf16[1024,1152]{0,1:T(8,128)(2,1)}, bf16[1024,1152]{0,1:T(8,128)(2,1)}, u32[]{:S(2)}, u32[]{:S(2)}) %collective-permute-start.1) | collective-permute-done | bytes 2359328 | tf_op jit(solution)/shard_map/ppermute | solution.py:12
  141.3 5.5 %convert_add_fusion = f32[1024,1152]{0,1:T(8,128)} fusion(bf16[1024,1152]{0,1:T(8,128)(2,1)} %collective-permute-done.1, bf16[512,1152]{0,1:T(8,128)(2,1)S(1)} %bitcast.36, f32[512,1024]{1,0:T(8,128)S(1)} %get-tuple-element.8, s32[512]{0:T(512)S(1)} %iota_add_fusion, f32[]{:T(128)} %bitcast.26), kind=kOutput, calls=%fused_computation.2 | convolution fusion | flops 1215037440 | bytes 10356740 | tf_op jit(solution)/shard_map/ij,ik->jk/dot_general | solution.py:68
  147.6 4.8 %fusion.13 = f32[512,1152]{1,0:T(8,128)S(1)} fusion(bf16[1024,1152]{0,1:T(8,128)(2,1)} %all-gather.2.cloned.1.call-done, f32[512,1024]{1,0:T(8,128)} %copy-done.8, s32[512]{0:T(512)} %copy-done.5, f32[]{:T(128)} %bitcast.21), kind=kOutput, calls=%fused_computation.37 | convolution fusion | flops 1212678144 | bytes 6817796 | tf_op jit(solution)/shard_map/dot_general | solution.py:60
  152.4 3.4 %fusion.4 = (f32[512]{0:T(512)S(1)}, f32[512,1152]{1,0:T(8,128)S(1)}) fusion(bf16[512,1152]{1,0:T(8,128)(2,1)S(1)} %copy.19, f32[512,1152]{1,0:T(8,128)S(1)} %fusion.13, bf16[1024,1152]{0,1:T(8,128)(2,1)} %collective-permute-done, f32[512,1024]{1,0:T(8,128)S(1)} %copy-done.7, f32[]{:T(128)} %bitcast.29, f32[]{:T(128)} %bitcast.22), kind=kOutput, calls=%fused_computation.17 | convolution fusion | flops 1213988352 | bytes 10356744 | tf_op jit(solution)/shard_map/dot_general | solution.py:62
  155.8 2.0 fusion.6
  157.8 2.0 copy.20
  159.8 3.9 %all-to-all-start.1 = ((f32[512,2,576]{0,2,1:T(8,128)}), f32[512,2,576]{0,2,1:T(8,128)S(1)}, u32[]{:S(2)}, u32[]{:S(2)}) async-start(f32[512,2,576]{0,2,1:T(8,128)} %bitcast.32), calls=%async_computation.1 | async-start | bytes 4718592 | tf_op jit(solution)/shard_map/all_to_all | solution.py:67
  164.3 52.5 %all-to-all-done.1 = f32[512,2,576]{0,2,1:T(8,128)S(1)} async-done(((f32[512,2,576]{0,2,1:T(8,128)}), f32[512,2,576]{0,2,1:T(8,128)S(1)}, u32[]{:S(2)}, u32[]{:S(2)}) %all-to-all-start.1) | async-done | bytes 2359328 | tf_op jit(solution)/shard_map/all_to_all | solution.py:67
  216.8 1.7 copy.25
  218.5 16.8 %reduce-scatter.2.cloned.1.call-done = f32[1024,576]{0,1:T(8,128)} async-done(((f32[1024,1152]{0,1:T(8,128)}), f32[1024,576]{0,1:T(8,128)}) %reduce-scatter.2.cloned.1.call-update) | async-done | bytes 2359312 | tf_op jit(solution)/shard_map/reduce_scatter | solution.py:75
  235.4 2.2 fusion.7
  237.5 3.8 %psum.23 = f32[1024]{0:T(1024)S(1)} all-reduce(f32[1024]{0:T(1024)S(1)} %fusion.7), channel_id=1, replica_groups=mesh['dp'=128,'mp'=2] {'mp'}, use_global_device_ids=true, to_apply=%region_7.8 | all-reduce | flops 1024 | bytes 8192 | tf_op jit(solution)/shard_map/psum | solution.py:77
  241.3 1.8 fusion.9
  (31 shorter events, 2.2 us)
Async XLA Ops:
  7.2 7.0 %copy-start = (bf16[1024,576]{0,1:T(8,128)(2,1)S(1)}, bf16[1024,576]{0,1:T(8,128)(2,1)}, u32[]{:S(2)}) copy-start(bf16[1024,576]{0,1:T(8,128)(2,1)} %param.5) | copy-start | bytes 3538948
  7.2 53.9 %all-gather.2.cloned.1.call-start = ((), (), s32[]{:S(2)}) async-start(), calls=%async_computation.3 | async-start | bytes 3538944 | tf_op jit(solution)/shard_map/all_gather | solution.py:28
  9.5 53.5 %copy-start.3 = (bf16[1024,576]{0,1:T(8,128)(2,1)S(1)}, bf16[1024,576]{0,1:T(8,128)(2,1)}, u32[]{:S(2)}) copy-start(bf16[1024,576]{0,1:T(8,128)(2,1)} %param.4) | copy-start | bytes 3538948
  61.1 44.4 %collective-permute-start = (bf16[1024,1152]{0,1:T(8,128)(2,1)}, bf16[1024,1152]{0,1:T(8,128)(2,1)}, u32[]{:S(2)}, u32[]{:S(2)}) collective-permute-start(bf16[1024,1152]{0,1:T(8,128)(2,1)} %all-gather.2.cloned.1.call-done), channel_id=1, source_target_pairs={{254,0},{0,2},{2,4},{4,6},{6,8},{8,10},{10,12},{12,14},{14,16},{16... | collective-permute-start | bytes 7077896 | tf_op jit(solution)/shard_map/ppermute | solution.py:12
  64.3 41.1 %all-to-all-start = ((bf16[2,512,576]{1,2,0:T(8,128)(2,1)}), bf16[2,512,576]{1,2,0:T(8,128)(2,1)S(1)}, u32[]{:S(2)}, u32[]{:S(2)}) async-start(bf16[2,512,576]{1,2,0:T(8,128)(2,1)} %bitcast.20), calls=%async_computation | async-start | bytes 2359296 | tf_op jit(solution)/shard_map/all_to_all | solution.py:27
  67.9 167.4 %reduce-scatter.2.cloned.1.call-start = ((), (), s32[]{:S(2)}) async-start(), calls=%async_computation.4 | async-start | bytes 7077888 | tf_op jit(solution)/shard_map/reduce_scatter | solution.py:75
  109.7 2.9 %copy-start.6 = (f32[512,1024]{1,0:T(8,128)}, f32[512,1024]{1,0:T(8,128)S(1)}, u32[]{:S(2)}) copy-start(f32[512,1024]{1,0:T(8,128)S(1)} %get-tuple-element.10) | copy-start | bytes 6291460
  112.7 28.6 %collective-permute-start.1 = (bf16[1024,1152]{0,1:T(8,128)(2,1)}, bf16[1024,1152]{0,1:T(8,128)(2,1)}, u32[]{:S(2)}, u32[]{:S(2)}) collective-permute-start(bf16[1024,1152]{0,1:T(8,128)(2,1)} %convolution_convert_fusion), channel_id=1, source_target_pairs={{2,0},{4,2},{6,4},{8,6},{10,8},{12,10},{14,12},{16,14},{18,16},{20... | collective-permute-start | bytes 7077896 | tf_op jit(solution)/shard_map/ppermute | solution.py:12
  113.1 33.7 %copy-start.5 = (s32[512]{0:T(512)}, s32[512]{0:T(512)S(1)}, u32[]{:S(2)}) copy-start(s32[512]{0:T(512)S(1)} %iota_add_fusion) | copy-start | bytes 6148
  118.3 22.9 %copy-start.8 = (f32[512,1024]{1,0:T(8,128)}, f32[512,1024]{1,0:T(8,128)S(1)}, u32[]{:S(2)}) copy-start(f32[512,1024]{1,0:T(8,128)S(1)} %get-tuple-element.8) | copy-start | bytes 6291460
  147.6 4.8 %copy-start.2 = (bf16[512,1152]{1,0:T(8,128)(2,1)}, bf16[512,1152]{1,0:T(8,128)(2,1)S(1)}, u32[]{:S(2)}) copy-start(bf16[512,1152]{1,0:T(8,128)(2,1)S(1)} %copy.19) | copy-start | bytes 3538948
  147.6 4.8 %copy-start.7 = (f32[512,1024]{1,0:T(8,128)S(1)}, f32[512,1024]{1,0:T(8,128)}, u32[]{:S(2)}) copy-start(f32[512,1024]{1,0:T(8,128)} %copy-done.6) | copy-start | bytes 6291460
  159.8 4.0 %copy-start.4 = (f32[512]{0:T(512)S(1)}, f32[512]{0:T(512)}, u32[]{:S(2)}) copy-start(f32[512]{0:T(512)} %get-tuple-element.7) | copy-start | bytes 6148
  159.8 57.0 %all-to-all-start.1 = ((f32[512,2,576]{0,2,1:T(8,128)}), f32[512,2,576]{0,2,1:T(8,128)S(1)}, u32[]{:S(2)}, u32[]{:S(2)}) async-start(f32[512,2,576]{0,2,1:T(8,128)} %bitcast.32), calls=%async_computation.1 | async-start | bytes 4718592 | tf_op jit(solution)/shard_map/all_to_all | solution.py:67
  235.4 6.0 %copy-start.1 = (f32[1024,576]{0,1:T(8,128)S(1)}, f32[1024,576]{0,1:T(8,128)}, u32[]{:S(2)}) copy-start(f32[1024,576]{0,1:T(8,128)} %reduce-scatter.2.cloned.1.call-done) | copy-start | bytes 7077892
Sparse Core Ops, SparseCore 0:
  15.6 45.4 all-gather.1
  147.0 88.3 reduce-scatter.1
where the time goes:
time: 251 us; the launch traced here: 250 us
  waiting for transfers between devices  174 us (69%)
  matrix products  26.1 us (10%)
  between operations  15.5 us (6%)
  other arithmetic  10.5 us (4%)
  starting transfers between devices  9.85 us (4%)
  blocking collectives  8.43 us (3%)
  local copies, waits for them, and re-layouts  5.56 us (2%)
    all_to_all x1, waiting for transfers between devices, per_device(): lax.all_to_all(image_local, 'mp', split_axis=1, concat_axis=0, tiled=True)  52.5 us
    all_gather x1, waiting for transfers between devices, per_device(): text_full = lax.all_gather(text_unit, 'mp', axis=1, tiled=True)  45.6 us
    all_to_all x1, waiting for transfers between devices, per_device(): lax.all_to_all(image_unit, 'mp', split_axis=0, concat_axis=1, tiled=True)  36.2 us
    ppermute x2, waiting for transfers between devices, shifted(): return lax.ppermute(block, axis, route)  22.9 us
    reduce_scatter x1, waiting for transfers between devices, per_device(): lax.psum_scatter(text_own + text_home, 'mp', scatter_dimension=1, tiled=T...  16.8 us
    dot_general x1, matrix products, per_device(): jnp.einsum('ij,ik->jk', local_block_weight, image_rows, preferred_element...  5.53 us
    dot_general x1, matrix products, per_device(): jnp.einsum('ik,jk->ij', image_rows, text_full, preferred_element_type=jnp...  5.25 us
  transfers between devices with their start and end apart: 6, of which 5 were waited for; matrix products, arithmetic and copies ran while one was open for 9% of the time, Pallas kernels for 0%

commit v1 on v0

v1 whole, which is shorter than its diff:
```python
import functools

import jax
import jax.numpy as jnp
from jax import lax
from jax.experimental import pallas as pl
from jax.experimental.pallas import tpu as pltpu
from jax.sharding import PartitionSpec as P

MESH = pl.DeviceIdType.MESH
F32 = jnp.float32
BF16 = jnp.bfloat16
EPSILON = 1e-06
LOG2E = 1.4426950408889634
TURN = 16
TILE_ROWS = 512
CHUNK = 256


def kernel(
    image,
    text,
    sharpness,
    offset,
    image_out,
    text_out,
    loss_out,
    image_raw,
    text_raw,
    image_unit,
    image_rows,
    text_unit,
    image_acc,
    text_acc,
    far_send,
    far_recv,
    dots,
    far_dots,
    row_dots,
    products,
    logs,
    image_inverse,
    text_inverse,
    image_ss,
    image_rs,
    text_ss,
    text_rs,
    whole_ss,
    whole_rs,
    pass_ss,
    pass_rs,
    far_ss,
    far_rs,
    dot_ss,
    dot_rs,
    local_sem,
    out_sem,
    go_sem,
):
    half, rows = image.shape
    chunks = rows // CHUNK
    halves = rows // TILE_ROWS
    blocks = lax.axis_size("dp")
    dp = lax.axis_index("dp")
    mp = lax.axis_index("mp")
    core = lax.rem(dp, 2)
    turn_next = (lax.rem(dp, TURN) == TURN - 1).astype(jnp.int32)
    turn_prev = (lax.rem(dp, TURN) == 0).astype(jnp.int32)
    partner = (dp, 1 - mp)
    following = (lax.rem(dp + 1, blocks), mp + turn_next * (1 - 2 * mp))
    preceding = (lax.rem(dp + blocks - 1, blocks), mp + turn_prev * (1 - 2 * mp))
    own_slot = 1 - core
    prev_slot = core
    prev_offset = pl.multiple_of(turn_prev * half, half)

    def span(start, size):
        return pl.ds(pl.multiple_of(start, size), size)

    def columns(j):
        return span(j * CHUNK, CHUNK)

    def remote(src, dst, send, recv, device):
        return pltpu.make_async_remote_copy(
            src_ref=src,
            dst_ref=dst,
            send_sem=send,
            recv_sem=recv,
            device_id=device,
            device_id_type=MESH,
        )

    def image_copy(j):
        return remote(
            image.at[:, columns(j)],
            image_raw.at[pl.ds(half, half), columns(j)],
            image_ss.at[j],
            image_rs.at[j],
            partner,
        )

    def text_copy(j):
        return remote(
            text.at[:, columns(j)],
            text_raw.at[own_slot, pl.ds(half, half), columns(j)],
            text_ss.at[j],
            text_rs.at[j],
            partner,
        )

    def whole_copy(slot, turned):
        return remote(
            text,
            text_raw.at[slot, span(turned * half, half), :],
            whole_ss.at[0],
            whole_rs.at[0],
            following,
        )

    def pass_copy(slot, turned, j):
        return remote(
            text_raw.at[own_slot, pl.ds(half, half), columns(j)],
            text_raw.at[slot, span((1 - turned) * half, half), columns(j)],
            pass_ss.at[j],
            pass_rs.at[j],
            following,
        )

    def far_copy(j):
        return remote(
            far_send.at[:, columns(j)],
            far_recv.at[:, columns(j)],
            far_ss.at[j],
            far_rs.at[j],
            preceding,
        )

    def dot_copy(j):
        return remote(
            dots.at[prev_slot, :, columns(j)],
            far_dots.at[:, columns(j)],
            dot_ss.at[j],
            dot_rs.at[j],
            preceding,
        )

    def image_here():
        return pltpu.make_async_copy(image, image_raw.at[pl.ds(0, half), :], local_sem.at[0])

    def text_here():
        return pltpu.make_async_copy(
            text, text_raw.at[own_slot, pl.ds(0, half), :], local_sem.at[1]
        )

    def image_result(j):
        return pltpu.make_async_copy(
            image_acc.at[:, columns(j)], image_out.at[:, columns(j)], out_sem.at[0, j]
        )

    def text_result(j):
        return pltpu.make_async_copy(
            text_acc.at[own_slot, :, columns(j)], text_out.at[:, columns(j)], out_sem.at[1, j]
        )

    def each(count, body):
        def step(j, carry):
            body(j)
            return carry

        lax.fori_loop(0, count, step, 0)

    scale = sharpness[0]
    slope = scale * LOG2E
    shift = offset[0] * LOG2E

    def normal(raw):
        values = raw.astype(F32)
        inverse = lax.rsqrt(jnp.sum(values * values, axis=0, keepdims=True) + EPSILON)
        return (values * inverse).astype(BF16), inverse

    def prepare_text(slot, j):
        unit, inverse = normal(text_raw[slot, :, columns(j)])
        text_unit[slot, :, columns(j)] = unit
        text_inverse[slot, 0:1, columns(j)] = inverse

    def prepare_image(j):
        unit, inverse = normal(image_raw[:, columns(j)])
        image_unit[:, columns(j)] = unit
        image_inverse[0:1, columns(j)] = inverse
        image_rows[columns(j), :] = unit.T

    def tile(slot, own, h, j, place):
        here = span(h * TILE_ROWS, TILE_ROWS)
        there = columns(j)
        dot = jnp.dot(image_rows[here, :], text_unit[slot, :, there], preferred_element_type=F32)
        power = dot * slope + shift
        if own:
            row = lax.broadcasted_iota(jnp.int32, dot.shape, 0) + h * TILE_ROWS
            column = lax.broadcasted_iota(jnp.int32, dot.shape, 1) + j * CHUNK
            paired = row == column
            power = jnp.where(paired, -power, power)
        term = jnp.exp2(power)
        total = term + 1.0
        weight = (term * scale) / total
        if own:
            weight = jnp.where(paired, -weight, weight)
        product = weight * dot
        row_dots[here, :] += product[:, :128] + product[:, 128:]
        products[here, :] *= total[:, :128] * total[:, 128:]
        dots[slot, 0:1, there] += jnp.sum(product, axis=0, keepdims=True)
        rounded = weight.astype(BF16)
        image_acc[:, here] += lax.dot_general(
            text_unit[slot, pl.ds(0, half), there],
            rounded,
            (((1,), (1,)), ((), ())),
            preferred_element_type=F32,
        )
        text_acc[slot, :, there] += jnp.dot(
            image_unit[pl.ds(place, half), here], rounded, preferred_element_type=F32
        )

    def take_logs():
        logs[...] += jnp.log(products[...])
        products[...] = jnp.ones_like(products)

    def send_far(slot, j):
        far_send[:, columns(j)] = text_acc[slot, :, columns(j)].astype(BF16)
        far_copy(j).start()
        dot_copy(j).start()

    def finish_image():
        image_dot = jnp.sum(row_dots[...].T, axis=0, keepdims=True)
        for j in range(chunks):
            cut = slice(j * CHUNK, (j + 1) * CHUNK)
            back = image_unit[0:half, cut].astype(F32)
            image_acc[:, cut] = (image_acc[:, cut] - back * image_dot[:, cut]) * image_inverse[
                0:1, cut
            ]
            image_result(j).start()

    def finish_loss():
        take_logs()
        image_inverse[0:1, :] = jnp.sum(logs[...].T, axis=0, keepdims=True) / (2 * rows)
        share = rows // 2
        loss_out[...] = image_inverse[0:1, span(mp * share, share)]

    def finish_text(slot, j):
        cut = columns(j)
        far_copy(j).wait_recv()
        dot_copy(j).wait_recv()
        total = text_acc[slot, :, cut] + far_recv[:, cut].astype(F32)
        dot = dots[slot, 0:1, cut] + far_dots[0:1, cut]
        back = text_unit[slot, pl.ds(0, half), cut].astype(F32)
        text_acc[slot, :, cut] = (total - back * dot) * text_inverse[slot, 0:1, cut]
        text_result(j).start()

    image_here().start()
    text_here().start()
    barrier = pltpu.get_barrier_semaphore()
    for device in (partner, following, preceding):
        pl.semaphore_signal(barrier, inc=1, device_id=device, device_id_type=MESH)
    pl.semaphore_wait(barrier, 3)

    @pl.when(core == 0)
    def _():
        each(chunks, lambda j: image_copy(j).start())

    @pl.when(core == 1)
    def _():
        each(chunks, lambda j: text_copy(j).start())
        each(chunks, lambda j: image_copy(j).start())

    whole_copy(own_slot, turn_next).start()

    image_acc[...] = jnp.zeros_like(image_acc)
    text_acc[...] = jnp.zeros_like(text_acc)
    dots[...] = jnp.zeros_like(dots)
    row_dots[...] = jnp.zeros_like(row_dots)
    logs[...] = jnp.zeros_like(logs)
    products[...] = jnp.ones_like(products)
    image_here().wait()
    text_here().wait()

    @pl.when(core == 0)
    def _():
        whole_copy(prev_slot, turn_prev).wait_recv()

        def ready(j):
            pass_copy(prev_slot, turn_prev, j).wait_recv()
            prepare_text(0, j)
            image_copy(j).wait_recv()
            prepare_image(j)

        each(chunks, ready)

        def first(j):
            each(halves, lambda h: tile(0, False, h, j, prev_offset))
            send_far(0, j)

        each(chunks, first)
        pl.semaphore_wait(go_sem, 1)
        each(chunks, lambda j: text_copy(j).start())
        take_logs()

        def second(j):
            text_copy(j).wait_recv()
            pass_copy(own_slot, turn_next, j).start()
            prepare_text(1, j)
            each(halves, lambda h: tile(1, True, h, j, 0))

        each(chunks, second)
        finish_image()
        finish_loss()
        each(chunks, lambda j: finish_text(1, j))

    @pl.when(core == 1)
    def _():
        def ready(j):
            text_copy(j).wait_recv()
            pass_copy(own_slot, turn_next, j).start()
            prepare_text(0, j)

        each(chunks, ready)

        per_half = TILE_ROWS // CHUNK

        def first(h):
            def arrive(i):
                image_copy(h * per_half + i).wait_recv()
                prepare_image(h * per_half + i)

            each(per_half, arrive)
            image_copy(h * per_half).wait_send()

            @pl.when(h == halves - 1)
            def _():
                pl.semaphore_signal(go_sem, inc=1, device_id=preceding, device_id_type=MESH)

            each(chunks, lambda j: tile(0, True, h, j, 0))

        each(halves, first)
        take_logs()
        whole_copy(prev_slot, turn_prev).wait_recv()

        def second(j):
            pass_copy(prev_slot, turn_prev, j).wait_recv()
            prepare_text(1, j)
            each(halves, lambda h: tile(1, False, h, j, 0))
            send_far(1, j)

        each(chunks, second)
        each(chunks, lambda j: finish_text(0, j))
        finish_image()
        finish_loss()

    def settle(j):
        text_copy(j).wait_send()
        pass_copy(own_slot, turn_next, j).wait_send()
        far_copy(j).wait_send()
        dot_copy(j).wait_send()
        image_result(j).wait()
        text_result(j).wait()

    each(chunks, settle)
    whole_copy(own_slot, turn_next).wait_send()

    @pl.when(core == 0)
    def _():
        each(chunks, lambda j: image_copy(j).wait_send())

    @pl.when(core == 1)
    def _():
        per_half = TILE_ROWS // CHUNK

        def rest(j):
            @pl.when(lax.rem(j, per_half) != 0)
            def _():
                image_copy(j).wait_send()

        each(chunks, rest)


def per_device(picture_vectors, caption_vectors, sharpness_coefficient, affinity_offset):
    rows, half = picture_vectors.shape
    chunks = rows // CHUNK
    width = 2 * half
    anywhere = pl.BlockSpec(memory_space=pl.ANY)
    scalar = pl.BlockSpec(memory_space=pltpu.SMEM)
    dma = pltpu.SemaphoreType.DMA
    image_grad, text_grad, row_loss = pl.pallas_call(
        kernel,
        out_shape=(
            jax.ShapeDtypeStruct((half, rows), F32),
            jax.ShapeDtypeStruct((half, rows), F32),
            jax.ShapeDtypeStruct((1, rows // 2), F32),
        ),
        in_specs=[anywhere, anywhere, scalar, scalar],
        out_specs=(anywhere, anywhere, pl.BlockSpec(memory_space=pltpu.VMEM)),
        scratch_shapes=[
            pltpu.VMEM((width, rows), BF16),
            pltpu.VMEM((2, width, rows), BF16),
            pltpu.VMEM((width, rows), BF16),
            pltpu.VMEM((rows, width), BF16),
            pltpu.VMEM((2, width, rows), BF16),
            pltpu.VMEM((half, rows), F32),
            pltpu.VMEM((2, half, rows), F32),
            pltpu.VMEM((half, rows), BF16),
            pltpu.VMEM((half, rows), BF16),
            pltpu.VMEM((2, 8, rows), F32),
            pltpu.VMEM((8, rows), F32),
            pltpu.VMEM((rows, 128), F32),
            pltpu.VMEM((rows, 128), F32),
            pltpu.VMEM((rows, 128), F32),
            pltpu.VMEM((8, rows), F32),
            pltpu.VMEM((2, 8, rows), F32),
            dma((chunks,)),
            dma((chunks,)),
            dma((chunks,)),
            dma((chunks,)),
            dma((1,)),
            dma((1,)),
            dma((chunks,)),
            dma((chunks,)),
            dma((chunks,)),
            dma((chunks,)),
            dma((chunks,)),
            dma((chunks,)),
            dma((2,)),
            dma((2, chunks)),
            pltpu.SemaphoreType.REGULAR,
        ],
        compiler_params=pltpu.CompilerParams(
            collective_id=0, has_side_effects=True, vmem_limit_bytes=48 * 1024 * 1024
        ),
        cost_estimate=pl.CostEstimate(
            flops=8 * rows * rows * width, bytes_accessed=12 * half * rows, transcendentals=0
        ),
    )(picture_vectors.T, caption_vectors.T, sharpness_coefficient, affinity_offset)
    return image_grad.T, text_grad.T, row_loss.reshape(rows // 2)


def solution(mesh):
    placed = (P("dp", "mp"), P("dp", "mp"), P(), P())
    return jax.shard_map(
        per_device,
        mesh=mesh,
        in_specs=placed,
        out_specs=(P("dp", "mp"), P("dp", "mp"), P(("dp", "mp"))),
        check_vma=False,
    )
```

time: 251 us -> 89 us (0.35)
  waiting for transfers between devices: 174 us -> 0 us
  Pallas kernels: 0 us -> 79.8 us
  matrix products: 26.1 us -> 0 us
  between operations: 15.5 us -> 1.95 us
  other arithmetic: 10.5 us -> 0 us
  starting transfers between devices: 9.85 us -> 0 us
  blocking collectives: 8.43 us -> 0 us
    all_to_all x2 -> x0, waiting for transfers between devices: 88.7 us -> none  [the longest x1 52.5 us: per_device(): lax.all_to_all(image_local, 'mp', split_axis=1, concat_axis=0, tiled=True)]
    pallas_call x0 -> x1, Pallas kernels: none -> 79.8 us  [per_device(): pl.pallas_call(kernel, out_shape=(jax.ShapeDtypeStruct((half, rows), F32)...]
    all_gather x1 -> x0, waiting for transfers between devices: 45.6 us -> none  [per_device(): text_full = lax.all_gather(text_unit, 'mp', axis=1, tiled=True)]
    dot_general x6 -> x0, matrix products: 26.1 us -> none  [the longest x1 5.53 us: per_device(): jnp.einsum('ij,ik->jk', local_block_weight, image_rows, preferred_element...]
    ppermute x2 -> x0, waiting for transfers between devices: 22.9 us -> none  [shifted(): return lax.ppermute(block, axis, route)]
    reduce_scatter x1 -> x0, waiting for transfers between devices: 16.8 us -> none  [per_device(): lax.psum_scatter(text_own + text_home, 'mp', scatter_dimension=1, tiled=T...]
    psum x2 -> x0, blocking collectives: 8.43 us -> none  [the longest x1 4.64 us: per_device(): lax.psum((jnp.sum(image_float * image_float, axis=1), jnp.sum(text_float...]
    all_to_all x2 -> x0, starting transfers between devices: 7.55 us -> none  [the longest x1 3.94 us: per_device(): lax.all_to_all(image_local, 'mp', split_axis=1, concat_axis=0, tiled=True)]
  transfers between devices with their start and end apart: 6 -> 0, of which waited for: 5 -> 0; matrix products, arithmetic and copies ran while one was open for 9% -> 0% of each run, Pallas kernels for 0% -> 0%
where the time goes in v1:
time: 89 us; the launch traced here: 88.8 us
  Pallas kernels  79.8 us (90%)
  local copies, waits for them, and re-layouts  7.03 us (8%)
  between operations  1.95 us (2%)
    pallas_call x1, Pallas kernels, per_device(): pl.pallas_call(kernel, out_shape=(jax.ShapeDtypeStruct((half, rows), F32)...  79.8 us
    unnamed x9, local copies, waits for them, and re-layouts  7.03 us

profile of v1, /device:TPU:1, one launch (start us, length us, event | category | flops | bytes accessed | tf_op | source)
XLA Modules:
  0.0 88.8 jit_solution(8224710388202375541)
XLA Ops:
  1.9 0.0 copy-start
  1.9 1.3 %copy-done = bf16[1024,576]{0,1:T(8,128)(2,1)S(1)} copy-done((bf16[1024,576]{0,1:T(8,128)(2,1)S(1)}, bf16[1024,576]{0,1:T(8,128)(2,1)}, u32[]{:S(2)}) %copy-start) | copy-done | bytes 1179672
  3.2 0.0 copy-start.1
  3.2 1.3 %copy-done.1 = bf16[1024,576]{0,1:T(8,128)(2,1)S(1)} copy-done((bf16[1024,576]{0,1:T(8,128)(2,1)S(1)}, bf16[1024,576]{0,1:T(8,128)(2,1)}, u32[]{:S(2)}) %copy-start.1) | copy-done | bytes 1179672
  4.5 79.8 %shard_map.67 = (f32[576,1024]{1,0:T(8,128)S(1)}, f32[576,1024]{1,0:T(8,128)}, f32[1,512]{1,0:T(1,128)S(1)}) custom-call(bf16[576,1024]{1,0:T(8,128)(2,1)S(1)} %bitcast.7, bf16[576,1024]{1,0:T(8,128)(2,1)S(1)} %bitcast.8, f32[1]{0:T(128)S(6)} %copy.10.sharpness, f32[1]{0:T(128)S(6)} %copy.11.offset), custom_call_target="tpu_custom_call" | custom-call | flops 9663676416 | bytes 7077888 | tf_op jit(solution)/shard_map/pallas_call | solution.py:389
  84.3 0.0 copy-start.2
  84.3 1.4 %copy.12 = f32[1024,576]{0,1:T(8,128)} copy(f32[1024,576]{0,1:T(8,128)S(1)} %bitcast.5) | data formatting | bytes 4718592
  85.7 1.1 %copy-done.2 = f32[576,1024]{1,0:T(8,128)S(1)} copy-done((f32[576,1024]{1,0:T(8,128)S(1)}, f32[576,1024]{1,0:T(8,128)}, u32[]{:S(2)}) %copy-start.2) | copy-done | bytes 2359320
  86.8 1.4 %copy.13 = f32[1024,576]{0,1:T(8,128)} copy(f32[1024,576]{0,1:T(8,128)S(1)} %bitcast.9) | data formatting | bytes 4718592
  88.2 0.6 copy.14
Async XLA Ops:
  1.9 1.3 %copy-start = (bf16[1024,576]{0,1:T(8,128)(2,1)S(1)}, bf16[1024,576]{0,1:T(8,128)(2,1)}, u32[]{:S(2)}) copy-start(bf16[1024,576]{0,1:T(8,128)(2,1)} %param.4) | copy-start | bytes 3538948
  3.2 1.3 %copy-start.1 = (bf16[1024,576]{0,1:T(8,128)(2,1)S(1)}, bf16[1024,576]{0,1:T(8,128)(2,1)}, u32[]{:S(2)}) copy-start(bf16[1024,576]{0,1:T(8,128)(2,1)} %param.5) | copy-start | bytes 3538948
  84.3 2.5 %copy-start.2 = (f32[576,1024]{1,0:T(8,128)S(1)}, f32[576,1024]{1,0:T(8,128)}, u32[]{:S(2)}) copy-start(f32[576,1024]{1,0:T(8,128)} %get-tuple-element.7) | copy-start | bytes 7077892

commit v2 on v1

--- a/solution.py
+++ b/solution.py
@@ -15,6 +15,7 @@
 TURN = 16
 TILE_ROWS = 512
 CHUNK = 256
+SMALL_PARTS = 4
 
 
 def kernel(
@@ -188,35 +189,47 @@
         image_inverse[0:1, columns(j)] = inverse
         image_rows[columns(j), :] = unit.T
 
-    def tile(slot, own, h, j, place):
-        here = span(h * TILE_ROWS, TILE_ROWS)
-        there = columns(j)
-        dot = jnp.dot(image_rows[here, :], text_unit[slot, :, there], preferred_element_type=F32)
-        power = dot * slope + shift
-        if own:
-            row = lax.broadcasted_iota(jnp.int32, dot.shape, 0) + h * TILE_ROWS
-            column = lax.broadcasted_iota(jnp.int32, dot.shape, 1) + j * CHUNK
-            paired = row == column
-            power = jnp.where(paired, -power, power)
-        term = jnp.exp2(power)
-        total = term + 1.0
-        weight = (term * scale) / total
-        if own:
-            weight = jnp.where(paired, -weight, weight)
-        product = weight * dot
-        row_dots[here, :] += product[:, :128] + product[:, 128:]
-        products[here, :] *= total[:, :128] * total[:, 128:]
-        dots[slot, 0:1, there] += jnp.sum(product, axis=0, keepdims=True)
-        rounded = weight.astype(BF16)
-        image_acc[:, here] += lax.dot_general(
-            text_unit[slot, pl.ds(0, half), there],
-            rounded,
-            (((1,), (1,)), ((), ())),
-            preferred_element_type=F32,
-        )
-        text_acc[slot, :, there] += jnp.dot(
-            image_unit[pl.ds(place, half), here], rounded, preferred_element_type=F32
-        )
+    def tile(slot, own, row, height, column, width, place, parts=1):
+        there = pl.ds(pl.multiple_of(column, CHUNK), width)
+        size = height // parts
+        spans = [pl.ds(pl.multiple_of(row + i * size, size), size) for i in range(parts)]
+        scores = [
+            jnp.dot(image_rows[here, :], text_unit[slot, :, there], preferred_element_type=F32)
+            for here in spans
+        ]
+        grads = []
+        inner = jnp.zeros((1, width), F32)
+        for i, (here, dot) in enumerate(zip(spans, scores)):
+            power = dot * slope + shift
+            if own:
+                first = lax.broadcasted_iota(jnp.int32, dot.shape, 0) + (row + i * size - column)
+                paired = first == lax.broadcasted_iota(jnp.int32, dot.shape, 1)
+                power = jnp.where(paired, -power, power)
+            term = jnp.exp2(power)
+            total = term + 1.0
+            weight = (term * scale) / total
+            if own:
+                weight = jnp.where(paired, -weight, weight)
+            product = weight * dot
+            summed, multiplied = product[:, :128], total[:, :128]
+            for lane in range(128, width, 128):
+                summed += product[:, lane : lane + 128]
+                multiplied *= total[:, lane : lane + 128]
+            row_dots[here, :] += summed
+            products[here, :] *= multiplied
+            inner += jnp.sum(product, axis=0, keepdims=True)
+            rounded = weight.astype(BF16)
+            image_acc[:, here] += lax.dot_general(
+                text_unit[slot, pl.ds(0, half), there],
+                rounded,
+                (((1,), (1,)), ((), ())),
+                preferred_element_type=F32,
+            )
+            grads.append(
+                jnp.dot(image_unit[pl.ds(place, half), here], rounded, preferred_element_type=F32)
+            )
+        dots[slot, 0:1, there] += inner
+        text_acc[slot, :, there] += sum(grads[1:], grads[0])
 
     def take_logs():
         logs[...] += jnp.log(products[...])
@@ -282,32 +295,40 @@
 
     @pl.when(core == 0)
     def _():
-        whole_copy(prev_slot, turn_prev).wait_recv()
-
-        def ready(j):
-            pass_copy(prev_slot, turn_prev, j).wait_recv()
-            prepare_text(0, j)
+        def arrive(j):
             image_copy(j).wait_recv()
             prepare_image(j)
 
-        each(chunks, ready)
-
-        def first(j):
-            each(halves, lambda h: tile(0, False, h, j, prev_offset))
-            send_far(0, j)
-
-        each(chunks, first)
+        each(chunks, arrive)
+        whole_copy(prev_slot, turn_prev).wait_recv()
+
+        def first(i):
+            def ready(j):
+                pass_copy(prev_slot, turn_prev, 2 * i + j).wait_recv()
+                prepare_text(0, 2 * i + j)
+
+            each(2, ready)
+            tile(0, False, 0, rows, 2 * i * CHUNK, 2 * CHUNK, prev_offset)
+            each(2, lambda j: send_far(0, 2 * i + j))
+
+        each(chunks // 2, first)
         pl.semaphore_wait(go_sem, 1)
         each(chunks, lambda j: text_copy(j).start())
         take_logs()
 
-        def second(j):
+        def ready(j):
             text_copy(j).wait_recv()
             pass_copy(own_slot, turn_next, j).start()
             prepare_text(1, j)
-            each(halves, lambda h: tile(1, True, h, j, 0))
-
-        each(chunks, second)
+
+        each(2, ready)
+        tile(1, True, 0, rows, 0, 2 * CHUNK, 0)
+
+        def second(j):
+            ready(j + 2)
+            tile(1, True, 0, rows, (j + 2) * CHUNK, CHUNK, 0, SMALL_PARTS)
+
+        each(chunks - 2, second)
         finish_image()
         finish_loss()
         each(chunks, lambda j: finish_text(1, j))
@@ -335,19 +356,29 @@
             def _():
                 pl.semaphore_signal(go_sem, inc=1, device_id=preceding, device_id_type=MESH)
 
-            each(chunks, lambda j: tile(0, True, h, j, 0))
+            each(
+                2,
+                lambda i: tile(0, True, h * TILE_ROWS, TILE_ROWS, 2 * i * CHUNK, 2 * CHUNK, 0),
+            )
 
         each(halves, first)
         take_logs()
         whole_copy(prev_slot, turn_prev).wait_recv()
 
-        def second(j):
+        def come(j):
             pass_copy(prev_slot, turn_prev, j).wait_recv()
             prepare_text(1, j)
-            each(halves, lambda h: tile(1, False, h, j, 0))
-            send_far(1, j)
-
-        each(chunks, second)
+
+        each(2, come)
+        tile(1, False, 0, rows, 0, 2 * CHUNK, 0)
+        each(2, lambda j: send_far(1, j))
+
+        def second(j):
+            come(j + 2)
+            tile(1, False, 0, rows, (j + 2) * CHUNK, CHUNK, 0, SMALL_PARTS)
+            send_far(1, j + 2)
+
+        each(chunks - 2, second)
         each(chunks, lambda j: finish_text(0, j))
         finish_image()
         finish_loss()
@@ -384,6 +415,7 @@
     chunks = rows // CHUNK
     width = 2 * half
     anywhere = pl.BlockSpec(memory_space=pl.ANY)
+    held = pl.BlockSpec(memory_space=pltpu.HBM)
     scalar = pl.BlockSpec(memory_space=pltpu.SMEM)
     dma = pltpu.SemaphoreType.DMA
     image_grad, text_grad, row_loss = pl.pallas_call(
@@ -393,7 +425,7 @@
             jax.ShapeDtypeStruct((half, rows), F32),
             jax.ShapeDtypeStruct((1, rows // 2), F32),
         ),
-        in_specs=[anywhere, anywhere, scalar, scalar],
+        in_specs=[held, held, scalar, scalar],
         out_specs=(anywhere, anywhere, pl.BlockSpec(memory_space=pltpu.VMEM)),
         scratch_shapes=[
             pltpu.VMEM((width, rows), BF16),
@@ -429,7 +461,7 @@
             pltpu.SemaphoreType.REGULAR,
         ],
         compiler_params=pltpu.CompilerParams(
-            collective_id=0, has_side_effects=True, vmem_limit_bytes=48 * 1024 * 1024
+            collective_id=0, has_side_effects=True, vmem_limit_bytes=60 * 1024 * 1024
         ),
         cost_estimate=pl.CostEstimate(
             flops=8 * rows * rows * width, bytes_accessed=12 * half * rows, transcendentals=0

time: 89 us -> 77.4 us (0.87)
  Pallas kernels: 79.8 us -> 69.8 us
  local copies, waits for them, and re-layouts: 7.03 us -> 5.5 us
    pallas_call x1, Pallas kernels: 79.8 us -> 69.8 us  [per_device(): pl.pallas_call(kernel, out_shape=(jax.ShapeDtypeStruct((half, rows), F32)...]
    unnamed x9 -> x7, local copies, waits for them, and re-layouts: 7.03 us -> 5.5 us
where the time goes in v2:
time: 77.4 us; the launch traced here: 77.3 us
  Pallas kernels  69.8 us (90%)
  local copies, waits for them, and re-layouts  5.5 us (7%)
  between operations  1.94 us (3%)
    pallas_call x1, Pallas kernels, per_device(): pl.pallas_call(kernel, out_shape=(jax.ShapeDtypeStruct((half, rows), F32)...  69.8 us
    unnamed x7, local copies, waits for them, and re-layouts  5.5 us

profile of v2, /device:TPU:1, one launch (start us, length us, event | category | flops | bytes accessed | tf_op | source)
XLA Modules:
  0.0 77.3 jit_solution(9200196314215092144)
XLA Ops:
  1.9 69.8 %shard_map.67 = (f32[576,1024]{1,0:T(8,128)}, f32[576,1024]{1,0:T(8,128)}, f32[1,512]{1,0:T(1,128)}) custom-call(bf16[576,1024]{1,0:T(8,128)(2,1)} %bitcast.8, bf16[576,1024]{1,0:T(8,128)(2,1)} %bitcast.9, f32[1]{0:T(128)S(6)} %copy.10.sharpness, f32[1]{0:T(128)S(6)} %copy.11.offset), custom_call_target="tpu_custom_call" | custom-call | flops 9663676416 | bytes 7077888 | tf_op jit(solution)/shard_map/pallas_call | solution.py:421
  71.7 0.0 copy-start
  71.8 3.5 %copy.12 = f32[1024,576]{0,1:T(8,128)} copy(f32[1024,576]{0,1:T(8,128)} %bitcast.6) | data formatting | bytes 4718592
  75.3 0.0 copy-done
  75.3 0.0 copy-start.1
  75.3 1.4 %copy.13 = f32[1024,576]{0,1:T(8,128)} copy(f32[1024,576]{0,1:T(8,128)S(1)} %bitcast.5) | data formatting | bytes 4718592
  76.7 0.0 copy-done.1
  76.7 0.6 copy.14
Async XLA Ops:
  71.7 3.5 %copy-start = (f32[576,1024]{1,0:T(8,128)S(1)}, f32[576,1024]{1,0:T(8,128)}, u32[]{:S(2)}) copy-start(f32[576,1024]{1,0:T(8,128)} %get-tuple-element.7) | copy-start | bytes 7077892
  75.3 1.4 %copy-start.1 = (f32[1,512]{1,0:T(1,128)S(1)}, f32[1,512]{1,0:T(1,128)}, u32[]{:S(2)}) copy-start(f32[1,512]{1,0:T(1,128)} %get-tuple-element.8) | copy-start | bytes 6148

commit v3 on v2

--- a/solution.py
+++ b/solution.py
@@ -16,6 +16,7 @@
 TILE_ROWS = 512
 CHUNK = 256
 SMALL_PARTS = 4
+STORES = 4
 
 
 def kernel(
@@ -327,11 +328,12 @@
         def second(j):
             ready(j + 2)
             tile(1, True, 0, rows, (j + 2) * CHUNK, CHUNK, 0, SMALL_PARTS)
+            finish_text(1, j)
 
         each(chunks - 2, second)
         finish_image()
         finish_loss()
-        each(chunks, lambda j: finish_text(1, j))
+        each(2, lambda j: finish_text(1, chunks - 2 + j))
 
     @pl.when(core == 1)
     def _():
@@ -345,17 +347,20 @@
         per_half = TILE_ROWS // CHUNK
 
         def first(h):
-            def arrive(i):
-                image_copy(h * per_half + i).wait_recv()
-                prepare_image(h * per_half + i)
-
-            each(per_half, arrive)
+            image_copy(h * per_half).wait_recv()
             image_copy(h * per_half).wait_send()
 
             @pl.when(h == halves - 1)
             def _():
                 pl.semaphore_signal(go_sem, inc=1, device_id=preceding, device_id_type=MESH)
 
+            prepare_image(h * per_half)
+
+            def arrive(i):
+                image_copy(h * per_half + i + 1).wait_recv()
+                prepare_image(h * per_half + i + 1)
+
+            each(per_half - 1, arrive)
             each(
                 2,
                 lambda i: tile(0, True, h * TILE_ROWS, TILE_ROWS, 2 * i * CHUNK, 2 * CHUNK, 0),
@@ -377,9 +382,9 @@
             come(j + 2)
             tile(1, False, 0, rows, (j + 2) * CHUNK, CHUNK, 0, SMALL_PARTS)
             send_far(1, j + 2)
+            each(2, lambda i: finish_text(0, 2 * j + i))
 
         each(chunks - 2, second)
-        each(chunks, lambda j: finish_text(0, j))
         finish_image()
         finish_loss()
 
@@ -410,12 +415,29 @@
         each(chunks, rest)
 
 
+def store(image_in, text_in, loss_in, image_out, text_out, loss_out, sem):
+    size = image_in.shape[0] // STORES
+    loss_out[...] = loss_in[...]
+    copies = []
+    for i in range(STORES):
+        part = pl.ds(i * size, size)
+        copies.append(pltpu.make_async_copy(image_in.at[part, :], image_out.at[part, :], sem.at[2 * i]))
+        copies.append(
+            pltpu.make_async_copy(text_in.at[part, :], text_out.at[part, :], sem.at[2 * i + 1])
+        )
+    for copy in copies:
+        copy.start()
+    for copy in copies:
+        copy.wait()
+
+
 def per_device(picture_vectors, caption_vectors, sharpness_coefficient, affinity_offset):
     rows, half = picture_vectors.shape
     chunks = rows // CHUNK
     width = 2 * half
     anywhere = pl.BlockSpec(memory_space=pl.ANY)
     held = pl.BlockSpec(memory_space=pltpu.HBM)
+    inside = pl.BlockSpec(memory_space=pltpu.VMEM)
     scalar = pl.BlockSpec(memory_space=pltpu.SMEM)
     dma = pltpu.SemaphoreType.DMA
     image_grad, text_grad, row_loss = pl.pallas_call(
@@ -461,12 +483,29 @@
             pltpu.SemaphoreType.REGULAR,
         ],
         compiler_params=pltpu.CompilerParams(
-            collective_id=0, has_side_effects=True, vmem_limit_bytes=60 * 1024 * 1024
+            collective_id=0, has_side_effects=True, vmem_limit_bytes=44 * 1024 * 1024
         ),
         cost_estimate=pl.CostEstimate(
             flops=8 * rows * rows * width, bytes_accessed=12 * half * rows, transcendentals=0
         ),
-    )(picture_vectors.T, caption_vectors.T, sharpness_coefficient, affinity_offset)
+    )(
+        pltpu.with_memory_space_constraint(picture_vectors.T, pltpu.HBM),
+        pltpu.with_memory_space_constraint(caption_vectors.T, pltpu.HBM),
+        sharpness_coefficient,
+        affinity_offset,
+    )
+    image_grad, text_grad, row_loss = pl.pallas_call(
+        store,
+        out_shape=(
+            jax.ShapeDtypeStruct((half, rows), F32),
+            jax.ShapeDtypeStruct((half, rows), F32),
+            jax.ShapeDtypeStruct((1, rows // 2), F32),
+        ),
+        in_specs=[anywhere, anywhere, inside],
+        out_specs=(anywhere, anywhere, inside),
+        scratch_shapes=[dma((2 * STORES,))],
+        compiler_params=pltpu.CompilerParams(vmem_limit_bytes=1024 * 1024),
+    )(image_grad, text_grad, row_loss)
     return image_grad.T, text_grad.T, row_loss.reshape(rows // 2)
 
 

time: 77.4 us -> 74.2 us (0.959)
  local copies, waits for them, and re-layouts: 5.5 us -> 0 us
  Pallas kernels: 69.8 us -> 72 us
    unnamed x7 -> x0, local copies, waits for them, and re-layouts: 5.5 us -> none
    pallas_call x0 -> x1, Pallas kernels: none -> 2.82 us  [per_device(): pl.pallas_call(store, out_shape=(jax.ShapeDtypeStruct((half, rows), F32),...]
where the time goes in v3:
time: 74.2 us; the launch traced here: 74 us
  Pallas kernels  72 us (97%)
  between operations  2.09 us (3%)
    pallas_call x1, Pallas kernels, per_device(): pl.pallas_call(kernel, out_shape=(jax.ShapeDtypeStruct((half, rows), F32)...  69.1 us
    pallas_call x1, Pallas kernels, per_device(): pl.pallas_call(store, out_shape=(jax.ShapeDtypeStruct((half, rows), F32),...  2.82 us

profile of v3, /device:TPU:1, one launch (start us, length us, event | category | flops | bytes accessed | tf_op | source)
XLA Modules:
  0.0 74.0 jit_solution(2145156190660447697)
XLA Ops:
  1.9 69.1 %shard_map.67 = (f32[576,1024]{1,0:T(8,128)S(1)}, f32[576,1024]{1,0:T(8,128)S(1)}, f32[1,512]{1,0:T(1,128)S(1)}) custom-call(bf16[576,1024]{1,0:T(8,128)(2,1)} %bitcast.7, bf16[576,1024]{1,0:T(8,128)(2,1)} %bitcast.8, f32[1]{0:T(128)S(6)} %copy.7.sharpness, f32[1]{0:T(128)S(6)} %copy.8.offset), custom_call_target="tpu_custom_call" | custom-call | flops 9663676416 | bytes 7077888 | tf_op jit(solution)/shard_map/pallas_call | solution.py:443
  71.1 2.8 %shard_map.68 = (f32[576,1024]{1,0:T(8,128)}, f32[576,1024]{1,0:T(8,128)}, f32[1,512]{1,0:T(1,128)}) custom-call(f32[576,1024]{1,0:T(8,128)S(1)} %get-tuple-element.9.image_in, f32[576,1024]{1,0:T(8,128)S(1)} %get-tuple-element.10.text_in, f32[1,512]{1,0:T(1,128)S(1)} %get-tuple-element.11.loss_in), custom_call_target="tpu_custom_call" | custom-call | tf_op jit(solution)/shard_map/pallas_call | solution.py:497

commit v4 on v3

--- a/solution.py
+++ b/solution.py
@@ -270,9 +270,9 @@
     image_here().start()
     text_here().start()
     barrier = pltpu.get_barrier_semaphore()
-    for device in (partner, following, preceding):
+    for device in (partner, preceding):
         pl.semaphore_signal(barrier, inc=1, device_id=device, device_id_type=MESH)
-    pl.semaphore_wait(barrier, 3)
+    pl.semaphore_wait(barrier, 2)
 
     @pl.when(core == 0)
     def _():
@@ -308,13 +308,16 @@
                 pass_copy(prev_slot, turn_prev, 2 * i + j).wait_recv()
                 prepare_text(0, 2 * i + j)
 
+            @pl.when(i == 1)
+            def _():
+                pl.semaphore_wait(go_sem, 1)
+                each(chunks, lambda j: text_copy(j).start())
+
             each(2, ready)
             tile(0, False, 0, rows, 2 * i * CHUNK, 2 * CHUNK, prev_offset)
             each(2, lambda j: send_far(0, 2 * i + j))
 
         each(chunks // 2, first)
-        pl.semaphore_wait(go_sem, 1)
-        each(chunks, lambda j: text_copy(j).start())
         take_logs()
 
         def ready(j):
@@ -343,6 +346,7 @@
             prepare_text(0, j)
 
         each(chunks, ready)
+        whole_copy(prev_slot, turn_prev).wait_recv()
 
         per_half = TILE_ROWS // CHUNK
 
@@ -368,7 +372,6 @@
 
         each(halves, first)
         take_logs()
-        whole_copy(prev_slot, turn_prev).wait_recv()
 
         def come(j):
             pass_copy(prev_slot, turn_prev, j).wait_recv()

time: 74.2 us -> 67.8 us (0.914)
  Pallas kernels: 72 us -> 65.6 us
    pallas_call x1, Pallas kernels: 69.1 us -> 62.8 us  [per_device(): pl.pallas_call(kernel, out_shape=(jax.ShapeDtypeStruct((half, rows), F32)...]
where the time goes in v4:
time: 67.8 us; the launch traced here: 67.7 us
  Pallas kernels  65.6 us (97%)
  between operations  2.09 us (3%)
    pallas_call x1, Pallas kernels, per_device(): pl.pallas_call(kernel, out_shape=(jax.ShapeDtypeStruct((half, rows), F32)...  62.8 us
    pallas_call x1, Pallas kernels, per_device(): pl.pallas_call(store, out_shape=(jax.ShapeDtypeStruct((half, rows), F32),...  2.82 us

profile of v4, /device:TPU:1, one launch (start us, length us, event | category | flops | bytes accessed | tf_op | source)
XLA Modules:
  0.0 67.7 jit_solution(5615153599947043046)
XLA Ops:
  1.9 62.8 %shard_map.67 = (f32[576,1024]{1,0:T(8,128)S(1)}, f32[576,1024]{1,0:T(8,128)S(1)}, f32[1,512]{1,0:T(1,128)S(1)}) custom-call(bf16[576,1024]{1,0:T(8,128)(2,1)} %bitcast.7, bf16[576,1024]{1,0:T(8,128)(2,1)} %bitcast.8, f32[1]{0:T(128)S(6)} %copy.7.sharpness, f32[1]{0:T(128)S(6)} %copy.8.offset), custom_call_target="tpu_custom_call" | custom-call | flops 9663676416 | bytes 7077888 | tf_op jit(solution)/shard_map/pallas_call | solution.py:446
  64.7 2.8 %shard_map.68 = (f32[576,1024]{1,0:T(8,128)}, f32[576,1024]{1,0:T(8,128)}, f32[1,512]{1,0:T(1,128)}) custom-call(f32[576,1024]{1,0:T(8,128)S(1)} %get-tuple-element.9.image_in, f32[576,1024]{1,0:T(8,128)S(1)} %get-tuple-element.10.text_in, f32[1,512]{1,0:T(1,128)S(1)} %get-tuple-element.11.loss_in), custom_call_target="tpu_custom_call" | custom-call | tf_op jit(solution)/shard_map/pallas_call | solution.py:500

commit v5 on v4

--- a/solution.py
+++ b/solution.py
@@ -56,7 +56,6 @@
     dot_ss,
     dot_rs,
     local_sem,
-    out_sem,
     go_sem,
 ):
     half, rows = image.shape
@@ -151,16 +150,6 @@
     def text_here():
         return pltpu.make_async_copy(
             text, text_raw.at[own_slot, pl.ds(0, half), :], local_sem.at[1]
-        )
-
-    def image_result(j):
-        return pltpu.make_async_copy(
-            image_acc.at[:, columns(j)], image_out.at[:, columns(j)], out_sem.at[0, j]
-        )
-
-    def text_result(j):
-        return pltpu.make_async_copy(
-            text_acc.at[own_slot, :, columns(j)], text_out.at[:, columns(j)], out_sem.at[1, j]
         )
 
     def each(count, body):
@@ -246,10 +235,9 @@
         for j in range(chunks):
             cut = slice(j * CHUNK, (j + 1) * CHUNK)
             back = image_unit[0:half, cut].astype(F32)
-            image_acc[:, cut] = (image_acc[:, cut] - back * image_dot[:, cut]) * image_inverse[
+            image_out[:, cut] = (image_acc[:, cut] - back * image_dot[:, cut]) * image_inverse[
                 0:1, cut
             ]
-            image_result(j).start()
 
     def finish_loss():
         take_logs()
@@ -264,11 +252,8 @@
         total = text_acc[slot, :, cut] + far_recv[:, cut].astype(F32)
         dot = dots[slot, 0:1, cut] + far_dots[0:1, cut]
         back = text_unit[slot, pl.ds(0, half), cut].astype(F32)
-        text_acc[slot, :, cut] = (total - back * dot) * text_inverse[slot, 0:1, cut]
-        text_result(j).start()
-
-    image_here().start()
-    text_here().start()
+        text_out[:, cut] = (total - back * dot) * text_inverse[slot, 0:1, cut]
+
     barrier = pltpu.get_barrier_semaphore()
     for device in (partner, preceding):
         pl.semaphore_signal(barrier, inc=1, device_id=device, device_id_type=MESH)
@@ -284,6 +269,8 @@
         each(chunks, lambda j: image_copy(j).start())
 
     whole_copy(own_slot, turn_next).start()
+    image_here().start()
+    text_here().start()
 
     image_acc[...] = jnp.zeros_like(image_acc)
     text_acc[...] = jnp.zeros_like(text_acc)
@@ -382,10 +369,10 @@
         each(2, lambda j: send_far(1, j))
 
         def second(j):
+            each(2, lambda i: finish_text(0, 2 * j + i))
             come(j + 2)
             tile(1, False, 0, rows, (j + 2) * CHUNK, CHUNK, 0, SMALL_PARTS)
             send_far(1, j + 2)
-            each(2, lambda i: finish_text(0, 2 * j + i))
 
         each(chunks - 2, second)
         finish_image()
@@ -396,8 +383,6 @@
         pass_copy(own_slot, turn_next, j).wait_send()
         far_copy(j).wait_send()
         dot_copy(j).wait_send()
-        image_result(j).wait()
-        text_result(j).wait()
 
     each(chunks, settle)
     whole_copy(own_slot, turn_next).wait_send()
@@ -451,7 +436,7 @@
             jax.ShapeDtypeStruct((1, rows // 2), F32),
         ),
         in_specs=[held, held, scalar, scalar],
-        out_specs=(anywhere, anywhere, pl.BlockSpec(memory_space=pltpu.VMEM)),
+        out_specs=(inside,) * 3,
         scratch_shapes=[
             pltpu.VMEM((width, rows), BF16),
             pltpu.VMEM((2, width, rows), BF16),
@@ -482,7 +467,6 @@
             dma((chunks,)),
             dma((chunks,)),
             dma((2,)),
-            dma((2, chunks)),
             pltpu.SemaphoreType.REGULAR,
         ],
         compiler_params=pltpu.CompilerParams(

time: 67.8 us -> 66.8 us (0.985)
  Pallas kernels: 65.6 us -> 64.6 us
    pallas_call x1, Pallas kernels: 62.8 us -> 61.7 us  [per_device(): pl.pallas_call(kernel, out_shape=(jax.ShapeDtypeStruct((half, rows), F32)...]
where the time goes in v5:
time: 66.8 us; the launch traced here: 66.7 us
  Pallas kernels  64.6 us (97%)
  between operations  2.09 us (3%)
    pallas_call x1, Pallas kernels, per_device(): pl.pallas_call(kernel, out_shape=(jax.ShapeDtypeStruct((half, rows), F32)...  61.7 us
    pallas_call x1, Pallas kernels, per_device(): pl.pallas_call(store, out_shape=(jax.ShapeDtypeStruct((half, rows), F32),...  2.82 us

profile of v5, /device:TPU:1, one launch (start us, length us, event | category | flops | bytes accessed | tf_op | source)
XLA Modules:
  0.0 66.7 jit_solution(9944458708860714301)
XLA Ops:
  1.9 61.7 %shard_map.67 = (f32[576,1024]{1,0:T(8,128)S(1)}, f32[576,1024]{1,0:T(8,128)S(1)}, f32[1,512]{1,0:T(1,128)S(1)}) custom-call(bf16[576,1024]{1,0:T(8,128)(2,1)} %bitcast.7, bf16[576,1024]{1,0:T(8,128)(2,1)} %bitcast.8, f32[1]{0:T(128)S(6)} %copy.7.sharpness, f32[1]{0:T(128)S(6)} %copy.8.offset), custom_call_target="tpu_custom_call" | custom-call | flops 9663676416 | bytes 7077888 | tf_op jit(solution)/shard_map/pallas_call | solution.py:431
  63.7 2.8 %shard_map.68 = (f32[576,1024]{1,0:T(8,128)}, f32[576,1024]{1,0:T(8,128)}, f32[1,512]{1,0:T(1,128)}) custom-call(f32[576,1024]{1,0:T(8,128)S(1)} %get-tuple-element.9.image_in, f32[576,1024]{1,0:T(8,128)S(1)} %get-tuple-element.10.text_in, f32[1,512]{1,0:T(1,128)S(1)} %get-tuple-element.11.loss_in), custom_call_target="tpu_custom_call" | custom-call | tf_op jit(solution)/shard_map/pallas_call | solution.py:484

commit v6 on v5

--- a/solution.py
+++ b/solution.py
@@ -13,7 +13,7 @@
 EPSILON = 1e-06
 LOG2E = 1.4426950408889634
 TURN = 16
-TILE_ROWS = 512
+TILE_ROWS = 256
 CHUNK = 256
 SMALL_PARTS = 4
 STORES = 4
@@ -341,7 +341,7 @@
             image_copy(h * per_half).wait_recv()
             image_copy(h * per_half).wait_send()
 
-            @pl.when(h == halves - 1)
+            @pl.when(h == 1)
             def _():
                 pl.semaphore_signal(go_sem, inc=1, device_id=preceding, device_id_type=MESH)
 

time: 66.8 us -> 66.7 us (level)
  no operation moved by 1% of the time
where the time goes in v6:
time: 66.7 us; the launch traced here: 66.6 us
  Pallas kernels  64.5 us (97%)
  between operations  2.09 us (3%)
    pallas_call x1, Pallas kernels, per_device(): pl.pallas_call(kernel, out_shape=(jax.ShapeDtypeStruct((half, rows), F32)...  61.6 us
    pallas_call x1, Pallas kernels, per_device(): pl.pallas_call(store, out_shape=(jax.ShapeDtypeStruct((half, rows), F32),...  2.82 us

profile of v6, /device:TPU:1, one launch (start us, length us, event | category | flops | bytes accessed | tf_op | source)
XLA Modules:
  0.0 66.6 jit_solution(12568711746742642681)
XLA Ops:
  1.9 61.6 %shard_map.67 = (f32[576,1024]{1,0:T(8,128)S(1)}, f32[576,1024]{1,0:T(8,128)S(1)}, f32[1,512]{1,0:T(1,128)S(1)}) custom-call(bf16[576,1024]{1,0:T(8,128)(2,1)} %bitcast.7, bf16[576,1024]{1,0:T(8,128)(2,1)} %bitcast.8, f32[1]{0:T(128)S(6)} %copy.7.sharpness, f32[1]{0:T(128)S(6)} %copy.8.offset), custom_call_target="tpu_custom_call" | custom-call | flops 9663676416 | bytes 7077888 | tf_op jit(solution)/shard_map/pallas_call | solution.py:431
  63.6 2.8 %shard_map.68 = (f32[576,1024]{1,0:T(8,128)}, f32[576,1024]{1,0:T(8,128)}, f32[1,512]{1,0:T(1,128)}) custom-call(f32[576,1024]{1,0:T(8,128)S(1)} %get-tuple-element.9.image_in, f32[576,1024]{1,0:T(8,128)S(1)} %get-tuple-element.10.text_in, f32[1,512]{1,0:T(1,128)S(1)} %get-tuple-element.11.loss_in), custom_call_target="tpu_custom_call" | custom-call | tf_op jit(solution)/shard_map/pallas_call | solution.py:484

commit v7 on v6

--- a/solution.py
+++ b/solution.py
@@ -16,7 +16,7 @@
 TILE_ROWS = 256
 CHUNK = 256
 SMALL_PARTS = 4
-STORES = 4
+STORES = 1
 
 
 def kernel(

time: 66.7 us -> 66.6 us (level)
  no operation moved by 1% of the time
where the time goes in v7:
time: 66.6 us; the launch traced here: 66.5 us
  Pallas kernels  64.4 us (97%)
  between operations  2.09 us (3%)
    pallas_call x1, Pallas kernels, per_device(): pl.pallas_call(kernel, out_shape=(jax.ShapeDtypeStruct((half, rows), F32)...  61.6 us
    pallas_call x1, Pallas kernels, per_device(): pl.pallas_call(store, out_shape=(jax.ShapeDtypeStruct((half, rows), F32),...  2.78 us

profile of v7, /device:TPU:1, one launch (start us, length us, event | category | flops | bytes accessed | tf_op | source)
XLA Modules:
  0.0 66.5 jit_solution(9234784786847348363)
XLA Ops:
  1.9 61.6 %shard_map.67 = (f32[576,1024]{1,0:T(8,128)S(1)}, f32[576,1024]{1,0:T(8,128)S(1)}, f32[1,512]{1,0:T(1,128)S(1)}) custom-call(bf16[576,1024]{1,0:T(8,128)(2,1)} %bitcast.7, bf16[576,1024]{1,0:T(8,128)(2,1)} %bitcast.8, f32[1]{0:T(128)S(6)} %copy.7.sharpness, f32[1]{0:T(128)S(6)} %copy.8.offset), custom_call_target="tpu_custom_call" | custom-call | flops 9663676416 | bytes 7077888 | tf_op jit(solution)/shard_map/pallas_call | solution.py:431
  63.6 2.8 %shard_map.68 = (f32[576,1024]{1,0:T(8,128)}, f32[576,1024]{1,0:T(8,128)}, f32[1,512]{1,0:T(1,128)}) custom-call(f32[576,1024]{1,0:T(8,128)S(1)} %get-tuple-element.9.image_in, f32[576,1024]{1,0:T(8,128)S(1)} %get-tuple-element.10.text_in, f32[1,512]{1,0:T(1,128)S(1)} %get-tuple-element.11.loss_in), custom_call_target="tpu_custom_call" | custom-call | tf_op jit(solution)/shard_map/pallas_call | solution.py:484
